TPU v7x, 32 devices: a whole 2x2x4 slice. The times are simulated.
32 devices in a mesh: fsdp: 4 (over y, x), dp: 8 (over z, core).
Axes of the slice: x: 2, y: 2, z: 4, core: 2. Of those that a mesh axis runs over, the one named last changes fastest.
Arguments:
- tokens: bfloat16 [4, 2112, 3200], P('fsdp', 'dp'), may hold values from -6 to 6
- norm_gain: float32 [3200], replicated, may hold values from 0.5 to 1.5
- qkv_weight: bfloat16 [3200, 3072], P('fsdp', 'dp'), may hold values from -4 to 4
- qk_gain: float32 [2, 1024], P(None, 'dp'), may hold values from 1 to 8
- out_weight: bfloat16 [1024, 3200], P('dp', 'fsdp'), may hold values from -0.1875 to 0.1875
- layer_scale: float32 [3200], replicated, may hold values from 0.2 to 1
- tile_counts: int32 [4, 2], replicated, may hold values from 0 to 2, as said below
- owners: int32 [4, 2], replicated, may hold values from 0 to 3, as said below
Outputs:
- vision_tokens: bfloat16 [16, 256, 12800], P('fsdp', None, 'dp')
Inputs may be any that keep to these rules, and one draw needn't show every extreme that they name: `tile_counts`: column 0 is 1 to 2, column 1 is 0 to 2 minus column 0. All owners together get at most 4 live tiles each, and one owner gets exactly 4.
All inputs are finite; a program needn't handle non-finite values.
Results may differ from a plain program's by a relative error of at most 0.006.
The roundings to bfloat16 on the way count: a program that leaves them out, or rounds other values in their place, can miss the bound.
Values may be sent and summed in bfloat16 or wider, within the bound.
A program may use at most 192 MiB of HBM per device.

v0:
```python
import jax
import jax.numpy as jnp
from jax import lax
from jax.sharding import PartitionSpec as P

HEAD_DIM = 128
GRID = 32
SLOTS = 2
TILE = 1025
CAP = 4


EPSILON = 1e-06


def merge_tiles(values):
    halves = GRID // 2
    columns = values.shape[1]
    tile_list = []
    for tile_slot in range(SLOTS):
        patches = values[tile_slot * TILE + 1 : (tile_slot + 1) * TILE]
        square = patches.reshape(halves, 2, halves, 2, columns).transpose(0, 2, 4, 1, 3)
        tile_list.append(square.reshape(halves * halves, columns * 4))
    return jnp.stack(tile_list)


def tile_owners(tile_counts, owners):
    slot_index = jnp.arange(SLOTS, dtype=jnp.int32)[None, :]
    first_count = tile_counts[:, 0:1]
    holder = jnp.where(slot_index < first_count, owners[:, 0:1], owners[:, 1:2])
    living = slot_index < first_count + tile_counts[:, 1:2]
    return (holder, living)


def place_tiles(received, holder, living, target):
    owned_flag = jnp.logical_and(living, holder == target).reshape(-1).astype(jnp.int32)
    before = jnp.cumsum(owned_flag) - owned_flag
    chosen = jnp.logical_and(
        before[None, :] == jnp.arange(CAP, dtype=jnp.int32)[:, None], owned_flag[None, :] == 1
    )
    flattened = received.reshape(received.shape[0] * received.shape[1], -1)
    placed = jnp.dot(chosen.astype(jnp.bfloat16), flattened, preferred_element_type=jnp.float32)
    return placed.astype(jnp.bfloat16).reshape(CAP, received.shape[2], received.shape[3])


def body(tokens, norm_gain, qkv_weight, qk_gain, out_weight, layer_scale, tile_counts, owners):
    own_rows = tokens[0]
    gathered = lax.all_gather(own_rows, "dp", axis=0, tiled=True)
    length = gathered.shape[0]
    model_width = gathered.shape[1]
    groups = lax.axis_size("dp")
    values = gathered.astype(jnp.float32)
    normed = (
        values * lax.rsqrt(jnp.mean(values * values, axis=-1, keepdims=True) + EPSILON) * norm_gain
    ).astype(jnp.bfloat16)
    projected = jnp.dot(
        normed,
        lax.all_gather(qkv_weight, "fsdp", axis=0, tiled=True),
        preferred_element_type=jnp.float32,
    )
    queries = projected[:, :HEAD_DIM]
    keys_part = projected[:, HEAD_DIM : 2 * HEAD_DIM]
    values_part = projected[:, 2 * HEAD_DIM :].astype(jnp.bfloat16)
    query_sums, key_sums = lax.psum(
        (jnp.sum(queries * queries, axis=-1), jnp.sum(keys_part * keys_part, axis=-1)), "dp"
    )
    window = groups * HEAD_DIM
    queries = (queries * lax.rsqrt(query_sums / window + EPSILON)[:, None] * qk_gain[0]).astype(
        jnp.bfloat16
    )
    keys_part = (keys_part * lax.rsqrt(key_sums / window + EPSILON)[:, None] * qk_gain[1]).astype(
        jnp.bfloat16
    )
    row_index = lax.axis_index("fsdp")
    row_count = lax.axis_size("fsdp")
    factor = HEAD_DIM ** (-0.5)
    covered = SLOTS * TILE
    tile_query = queries[:covered].reshape(SLOTS, TILE, HEAD_DIM)
    tile_key = keys_part[:covered].reshape(SLOTS, TILE, HEAD_DIM)
    tile_value = values_part[:covered].reshape(SLOTS, TILE, HEAD_DIM)
    scores = (
        jnp.einsum("sqc,skc->sqk", tile_query, tile_key, preferred_element_type=jnp.float32)
        * factor
    )
    highest = jnp.max(scores, axis=-1, keepdims=True)
    exponent = jnp.exp(scores - highest)
    weights = (exponent / jnp.sum(exponent, axis=-1, keepdims=True)).astype(jnp.bfloat16)
    tile_out = jnp.einsum(
        "sqk,skc->sqc", weights, tile_value, preferred_element_type=jnp.float32
    ).astype(jnp.bfloat16)
    head_out = jnp.concatenate(
        [
            tile_out.reshape(covered, HEAD_DIM),
            jnp.zeros((length - covered, HEAD_DIM), jnp.bfloat16),
        ],
        axis=0,
    )
    token_heads = lax.all_to_all(head_out, "dp", split_axis=0, concat_axis=1, tiled=True)
    weight_rows = lax.all_gather(out_weight, "dp", axis=0, tiled=True)
    weight_full = lax.all_gather(weight_rows, "fsdp", axis=1, tiled=True)
    rows_here = token_heads.shape[0]
    head_terms = jnp.einsum(
        "shc,hcd->shd",
        token_heads.reshape(rows_here, groups, HEAD_DIM),
        weight_full.reshape(groups, HEAD_DIM, model_width),
        preferred_element_type=jnp.float32,
    ).astype(jnp.bfloat16)
    attention = jnp.sum(lax.optimization_barrier(head_terms).astype(jnp.float32), axis=1)
    token_update = (own_rows.astype(jnp.float32) + layer_scale * attention).astype(jnp.bfloat16)
    updated = lax.all_to_all(token_update, "dp", split_axis=1, concat_axis=0, tiled=True)
    merged = merge_tiles(updated)
    holder, living = tile_owners(tile_counts, owners)
    own_holder = holder[row_index]
    own_living = living[row_index]
    destination = jnp.arange(row_count, dtype=jnp.int32)[:, None]
    sending = jnp.logical_and(destination == own_holder[None, :], own_living[None, :])
    outgoing = jnp.where(sending[:, :, None, None], merged[None], jnp.zeros((), jnp.bfloat16))
    received = lax.all_to_all(outgoing, "fsdp", split_axis=0, concat_axis=0, tiled=True)
    return place_tiles(received, holder, living, row_index)


def solution(mesh):
    placed = (
        P("fsdp", "dp", None),
        P(),
        P("fsdp", "dp"),
        P(None, "dp"),
        P("dp", "fsdp"),
        P(),
        P(),
        P(),
    )
    return jax.shard_map(
        body, mesh=mesh, in_specs=placed, out_specs=P("fsdp", None, "dp"), check_vma=False
    )
```

profile of v0, /device:TPU:0, one launch (start us, length us, event | category | flops | bytes accessed | tf_op | source)
XLA Modules:
  0.0 553.2 jit_solution(6117920376417589378)
XLA Ops:
  6.5 0.7 all-gather.8.cloned.1.call-update
  7.3 0.7 all-gather.12.cloned.1.call-update
  8.1 0.7 all-gather.6.cloned.1.call-update
  8.8 30.5 %all-gather.8.cloned.1.call-done = bf16[1024,800]{0,1:T(8,128)(2,1)} async-done(((bf16[128,800]{0,1:T(8,128)(2,1)}), bf16[1024,800]{0,1:T(8,128)(2,1)}) %all-gather.8.cloned.1.call-update) | async-done | bytes 1638416 | tf_op jit(solution)/shard_map/all_gather | solution.py:99
  39.3 0.8 slice_bitcast_fusion
  40.0 124.5 %all-gather.12.cloned.1.call-done = bf16[1,2112,3200]{2,1,0:T(8,128)(2,1)} async-done(((bf16[1,264,3200]{2,1,0:T(8,128)(2,1)}), bf16[1,2112,3200]{2,1,0:T(8,128)(2,1)}) %all-gather.12.cloned.1.call-update) | async-done | bytes 13516816 | tf_op jit(solution)/shard_map/all_gather | solution.py:48
  164.6 7.5 %fusion.1 = f32[2112]{0:T(1024)S(1)} fusion(bf16[1,2112,3200]{2,1,0:T(8,128)(2,1)} %all-gather.12.cloned.1.call-done), kind=kLoop, calls=%fused_computation.4 | loop fusion | flops 20273088 | bytes 13525248 | tf_op jit(solution)/shard_map/reduce_sum | solution.py:54
  172.1 30.8 %all-gather.6.cloned.1.call-done = bf16[3200,384]{1,0:T(8,128)(2,1)} async-done(((bf16[800,384]{1,0:T(8,128)(2,1)}), bf16[3200,384]{1,0:T(8,128)(2,1)}) %all-gather.6.cloned.1.call-update) | async-done | bytes 2457616 | tf_op jit(solution)/shard_map/all_gather | solution.py:58
  203.0 11.3 %fusion.5 = f32[2112,384]{1,0:T(8,128)S(1)} fusion(bf16[3200,384]{1,0:T(8,128)(2,1)} %all-gather.6.cloned.1.call-done, bf16[1,2112,3200]{2,1,0:T(8,128)(2,1)} %all-gather.12.cloned.1.call-done, f32[3200]{0:T(1024)S(1)} %copy-done.5, f32[2112]{0:T(1024)S(1)} %add_rsqrt_fusion.2), kind=kOutput, calls=%fused_computation.10 | convolution fusion | flops 5217484800 | bytes 19239680 | tf_op jit(solution)/shard_map/dot_general | solution.py:56
  214.2 0.9 slice.84
  215.1 0.6 multiply_reduce_fusion
  215.7 29.2 %all-reduce.1 = (f32[2112]{0:T(1024)S(1)}, f32[2112]{0:T(1024)S(1)}) all-reduce(f32[2112]{0:T(1024)S(1)} %get-tuple-element.6, f32[2112]{0:T(1024)S(1)} %get-tuple-element.5), channel_id=1, replica_groups=mesh['fsdp'=4,'dp'=8] {'dp'}, use_global_device_ids=true, to_apply=%region_3.0 | all-reduce | flops 4224 | bytes 33792 | tf_op jit(solution)/shard_map/psum | solution.py:64
  245.0 1.2 fusion.14
  246.4 1.2 reshape.258
  247.7 3.2 fusion.30
  250.9 6.8 %fusion.12 = bf16[2,1025,128]{2,1,0:T(8,128)(2,1)} fusion(bf16[2,1025,128]{2,1,0:T(8,128)(2,1)S(1)} %reshape.258, f32[2,1025]{1,0:T(2,128)S(1)} %fusion.30, bf16[2,1025,128]{2,1,0:T(8,128)(2,1)} %copy-done.1, bf16[2,1025,128]{2,1,0:T(8,128)(2,1)S(1)} %reshape.257), kind=kOutput, calls=%fused_computation.20 | convolution fusion | flops 1084510464 | bytes 2107400 | tf_op jit(solution)/shard_map/sqk,skc->sqc/dot_general | solution.py:88
  257.7 1.2 reshape.259
  258.9 0.8 concatenate.3
  259.7 3.7 all-to-all-start
  263.5 6.0 %reshape.267 = f32[264,8,400]{2,1,0:T(8,128)} reshape(bf16[1,264,3200]{2,1,0:T(8,128)(2,1)S(1)} %copy-done) | data formatting | bytes 5068800 | tf_op jit(solution)/shard_map/convert_element_type | solution.py:109
  269.6 7.4 %all-gather.10.cloned.1.call-done = bf16[1024,3200]{0,1:T(8,128)(2,1)} async-done(((bf16[1024,800]{0,1:T(8,128)(2,1)}), bf16[1024,3200]{0,1:T(8,128)(2,1)}) %all-gather.10.cloned.1.call-update) | async-done | bytes 6553616 | tf_op jit(solution)/shard_map/all_gather | solution.py:100
  277.0 9.2 %copy.27 = bf16[1024,3200]{1,0:T(8,128)(2,1)} copy(bf16[1024,3200]{0,1:T(8,128)(2,1)} %all-gather.10.cloned.1.call-done) | data formatting | bytes 13107200 | tf_op jit(solution)/shard_map/all_gather | solution.py:100
  286.3 9.7 %convert_bitcast_fusion = bf16[264,8,3200]{2,0,1:T(8,128)(2,1)} fusion(bf16[8,128,3200]{2,1,0:T(8,128)(2,1)} %bitcast.57, bf16[8,264,128]{2,1,0:T(8,128)(2,1)S(1)} %all-to-all-done), kind=kOutput, calls=%fused_computation.12 | convolution fusion | flops 1736908800 | bytes 20611072 | tf_op jit(solution)/shard_map/shc,hcd->shd/dot_general | solution.py:102
  295.9 7.0 %convert_reduce_fusion = f32[264,3200]{1,0:T(8,128)S(1)} fusion(bf16[264,8,3200]{2,0,1:T(8,128)(2,1)} %convert_bitcast_fusion), kind=kLoop, calls=%fused_computation.7 | loop fusion | flops 12672000 | bytes 16896000 | tf_op jit(solution)/shard_map/reduce_sum | solution.py:108
  303.0 5.4 reduce_sum.52
  308.4 4.7 add_convert_fusion
  313.1 2.1 copy.28
  315.2 4.8 all-to-all-start.1
  320.3 50.2 %all-to-all-done.1 = bf16[264,8,400]{2,0,1:T(8,128)(2,1)S(1)} async-done(((bf16[264,8,400]{2,0,1:T(8,128)(2,1)}), bf16[264,8,400]{2,0,1:T(8,128)(2,1)S(1)}, u32[]{:S(2)}, u32[]{:S(2)}) %all-to-all-start.1) | async-done | bytes 1689632 | tf_op jit(solution)/shard_map/all_to_all | solution.py:110
  370.5 1.5 fusion.29
  371.9 1.5 reshape.261
  373.5 12.3 %copy.29 = bf16[16,16,400,2,2]{1,0,4,3,2:T(8,128)(2,1)} copy(bf16[16,16,400,2,2]{2,4,1,3,0:T(2,128)(2,1)S(1)} %bitcast.59) | data formatting | bytes 1638400 | tf_op jit(solution)/shard_map/transpose | solution.py:22
  385.7 8.1 %stack_reshape.6 = bf16[1,256,1600]{1,2,0:T(8,128)(2,1)S(1)} reshape(bf16[16,16,400,2,2]{1,0,4,3,2:T(8,128)(2,1)} %copy.29) | data formatting | bytes 1638400 | tf_op jit(solution)/shard_map/stack;reshape | solution.py:24
  393.8 0.5 reshape.262
  394.3 12.3 %copy.30 = bf16[16,16,400,2,2]{1,0,4,3,2:T(8,128)(2,1)} copy(bf16[16,16,400,2,2]{2,4,1,3,0:T(2,128)(2,1)S(1)} %bitcast.60) | data formatting | bytes 1638400 | tf_op jit(solution)/shard_map/transpose | solution.py:22
  406.6 8.1 %stack_reshape.7 = bf16[1,256,1600]{1,2,0:T(8,128)(2,1)S(1)} reshape(bf16[16,16,400,2,2]{1,0,4,3,2:T(8,128)(2,1)} %copy.30) | data formatting | bytes 1638400 | tf_op jit(solution)/shard_map/stack;reshape | solution.py:24
  414.7 0.2 pad_maximum_fusion
  414.9 3.2 broadcast_select_fusion
  418.1 5.6 %all-to-all-start.2 = ((bf16[4,2,256,1600]{2,3,1,0:T(8,128)(2,1)}), bf16[4,2,256,1600]{2,3,1,0:T(8,128)(2,1)}, u32[]{:S(2)}, u32[]{:S(2)}) async-start(bf16[4,2,256,1600]{2,3,1,0:T(8,128)(2,1)} %broadcast_select_fusion), calls=%async_computation.2 | async-start | bytes 13107200 | tf_op jit(solution)/shard_map/all_to_all | solution.py:118
  423.8 0.2 reduce-window.8
  424.0 72.4 %all-to-all-done.2 = bf16[4,2,256,1600]{2,3,1,0:T(8,128)(2,1)} async-done(((bf16[4,2,256,1600]{2,3,1,0:T(8,128)(2,1)}), bf16[4,2,256,1600]{2,3,1,0:T(8,128)(2,1)}, u32[]{:S(2)}, u32[]{:S(2)}) %all-to-all-start.2) | async-done | bytes 6553632 | tf_op jit(solution)/shard_map/all_to_all | solution.py:118
  496.4 9.7 %copy.31 = bf16[4,2,256,1600]{3,2,1,0:T(8,128)(2,1)} copy(bf16[4,2,256,1600]{2,3,1,0:T(8,128)(2,1)} %all-to-all-done.2) | data formatting | bytes 13107200 | tf_op jit(solution)/shard_map/all_to_all | solution.py:118
  506.1 13.5 %reshape.270 = bf16[3276800]{0:T(1024)(128)(2,1)} reshape(bf16[4,2,256,1600]{3,2,1,0:T(8,128)(2,1)} %copy.31) | data formatting | bytes 13107200
  519.7 8.3 %reshape.263 = bf16[8,409600]{1,0:T(8,128)(2,1)} reshape(bf16[3276800]{0:T(1024)(128)(2,1)} %reshape.270) | data formatting | bytes 13107200 | tf_op jit(solution)/shard_map/reshape | solution.py:41
  528.0 4.7 convolution_convert_fusion
  532.7 5.0 reshape.272
  537.7 5.1 reshape.264
  542.8 3.6 copy.32
  (34 shorter events, 0.8 us)
Async XLA Ops:
  6.5 32.7 %all-gather.8.cloned.1.call-start = ((), (), s32[]{:S(2)}) async-start(), calls=%async_computation.4 | async-start | bytes 1843200 | tf_op jit(solution)/shard_map/all_gather | solution.py:99
  7.3 157.3 %all-gather.12.cloned.1.call-start = ((), (), s32[]{:S(2)}) async-start(), calls=%async_computation.6 | async-start | bytes 15206400 | tf_op jit(solution)/shard_map/all_gather | solution.py:48
  8.0 194.9 %all-gather.6.cloned.1.call-start = ((), (), s32[]{:S(2)}) async-start(), calls=%async_computation.3 | async-start | bytes 3072000 | tf_op jit(solution)/shard_map/all_gather | solution.py:58
  8.7 268.3 %all-gather.10.cloned.1.call-start = ((), (), s32[]{:S(2)}) async-start(), calls=%async_computation.5 | async-start | bytes 8192000 | tf_op jit(solution)/shard_map/all_gather | solution.py:100
  40.0 162.9 %copy-start.5 = (f32[3200]{0:T(1024)S(1)}, f32[3200]{0:T(1024)}, u32[]{:S(2)}) copy-start(f32[3200]{0:T(1024)} %param.9) | copy-start | bytes 38404
  246.3 1.4 copy-start.1
  250.9 12.6 %copy-start = (bf16[1,264,3200]{2,1,0:T(8,128)(2,1)S(1)}, bf16[1,264,3200]{2,1,0:T(8,128)(2,1)}, u32[]{:S(2)}) copy-start(bf16[1,264,3200]{2,1,0:T(8,128)(2,1)} %param.8) | copy-start | bytes 5068804
  257.7 11.8 %copy-start.2 = (f32[3200]{0:T(1024)S(1)}, f32[3200]{0:T(1024)}, u32[]{:S(2)}) copy-start(f32[3200]{0:T(1024)} %param.13) | copy-start | bytes 38404
  259.7 26.5 %all-to-all-start = ((bf16[8,264,128]{2,1,0:T(8,128)(2,1)}), bf16[8,264,128]{2,1,0:T(8,128)(2,1)S(1)}, u32[]{:S(2)}, u32[]{:S(2)}) async-start(bf16[8,264,128]{2,1,0:T(8,128)(2,1)} %bitcast.11), calls=%async_computation | async-start | bytes 1081344 | tf_op jit(solution)/shard_map/all_to_all | solution.py:98
  313.1 7.0 %copy-start.3 = (s32[4,2]{0,1:T(2,128)S(1)}, s32[4,2]{0,1:T(2,128)}, u32[]{:S(2)}) copy-start(s32[4,2]{0,1:T(2,128)} %param.15) | copy-start | bytes 100
  313.1 7.0 %copy-start.4 = (s32[4,2]{0,1:T(2,128)S(1)}, s32[4,2]{0,1:T(2,128)}, u32[]{:S(2)}) copy-start(s32[4,2]{0,1:T(2,128)} %param.14) | copy-start | bytes 100
  315.2 55.3 %all-to-all-start.1 = ((bf16[264,8,400]{2,0,1:T(8,128)(2,1)}), bf16[264,8,400]{2,0,1:T(8,128)(2,1)S(1)}, u32[]{:S(2)}, u32[]{:S(2)}) async-start(bf16[264,8,400]{2,0,1:T(8,128)(2,1)} %copy.28), calls=%async_computation.1 | async-start | bytes 4325376 | tf_op jit(solution)/shard_map/all_to_all | solution.py:110
  418.1 78.3 %all-to-all-start.2 = ((bf16[4,2,256,1600]{2,3,1,0:T(8,128)(2,1)}), bf16[4,2,256,1600]{2,3,1,0:T(8,128)(2,1)}, u32[]{:S(2)}, u32[]{:S(2)}) async-start(bf16[4,2,256,1600]{2,3,1,0:T(8,128)(2,1)} %broadcast_select_fusion), calls=%async_computation.2 | async-start | bytes 13107200 | tf_op jit(solution)/shard_map/all_to_all | solution.py:118
Sparse Core Ops, SparseCore 0:
  8.9 30.2 all-gather.7
  40.9 123.6 all-gather.11
  166.4 36.5 all-gather.5
  204.7 72.3 all-gather.9
where the time goes:
time: 560 us; the launch traced here: 553 us
  waiting for transfers between devices  318 us (57%)
  local copies, waits for them, and re-layouts  118 us (21%)
  matrix products  35.7 us (6%)
  blocking collectives  29.2 us (5%)
  other arithmetic  24.8 us (4%)
  starting transfers between devices  14.2 us (3%)
  between operations  13.6 us (2%)
    all_gather x1, waiting for transfers between devices, body(): gathered = lax.all_gather(own_rows, 'dp', axis=0, tiled=True)  125 us
    all_to_all x1, waiting for transfers between devices, body(): lax.all_to_all(outgoing, 'fsdp', split_axis=0, concat_axis=0, tiled=True)  72.4 us
    all_to_all x1, waiting for transfers between devices, body(): lax.all_to_all(token_update, 'dp', split_axis=1, concat_axis=0, tiled=True)  50.2 us
    all_gather x1, waiting for transfers between devices, body(): lax.all_gather(qkv_weight, 'fsdp', axis=0, tiled=True)  30.8 us
    all_gather x1, waiting for transfers between devices, body(): weight_rows = lax.all_gather(out_weight, 'dp', axis=0, tiled=True)  30.5 us
    psum x1, blocking collectives, body(): lax.psum((jnp.sum(queries * queries, axis=-1), jnp.sum(keys_part * keys_p...  29.2 us
    transpose x2, local copies, waits for them, and re-layouts, merge_tiles(): patches.reshape(halves, 2, halves, 2, columns).transpose(0, 2, 4, 1, 3)  24.5 us
    unnamed x14, local copies, waits for them, and re-layouts  18.6 us
  transfers between devices with their start and end apart: 7, of which 6 were waited for; matrix products, arithmetic and copies ran while one was open for 9% of the time, Pallas kernels for 0%

commit v1 on v0

v1 whole, which is shorter than its diff:
```python
import jax
import jax.numpy as jnp
from jax import lax
from jax.experimental import pallas as pl
from jax.experimental.pallas import tpu as pltpu
from jax.sharding import PartitionSpec as P

HEAD_DIM = 128
GRID = 32
SLOTS = 2
TILE = 1025
CAP = 4
HALF = GRID // 2
CELLS = HALF * HALF
EPSILON = 1e-06


def patch_order(values):
    columns = values.shape[-1]
    square = values.reshape(HALF, 2, HALF, 2, columns).transpose(1, 3, 0, 2, 4)
    return square.reshape(4 * CELLS, columns)


def project_kernel(att_ref, weight_ref, token_ref, scale_ref, out_ref):
    places, rows, _ = token_ref.shape
    width = token_ref.shape[2]
    groups = att_ref.shape[0]
    total = jnp.zeros((places * rows, width), jnp.float32)
    for group in range(groups):
        for part in range(2):
            block = att_ref[group, :, :, part * HEAD_DIM : (part + 1) * HEAD_DIM]
            term = jnp.dot(
                block.reshape(places * rows, HEAD_DIM),
                weight_ref[part * groups + group],
                preferred_element_type=jnp.float32,
            )
            total = total + term.astype(jnp.bfloat16).astype(jnp.float32)
    tokens = token_ref[...].reshape(places * rows, width).astype(jnp.float32)
    updated = (tokens + scale_ref[...] * total).astype(jnp.bfloat16)
    for start in range(0, width, 128):
        size = min(128, width - start)
        feature = lax.broadcasted_iota(jnp.int32, (size, 4 * size), 0)
        lane = lax.broadcasted_iota(jnp.int32, (size, 4 * size), 1)
        merged = jnp.zeros((rows, 4 * size), jnp.float32)
        for place in range(4):
            spread = jnp.where(lane == 4 * feature + place, 1.0, 0.0).astype(jnp.bfloat16)
            merged = merged + jnp.dot(
                updated[place * rows : (place + 1) * rows, start : start + size],
                spread,
                preferred_element_type=jnp.float32,
            )
        out_ref[:, 4 * start : 4 * (start + size)] = merged.astype(jnp.bfloat16)


def project_merge(attended, weight, tokens, scale):
    groups = attended.shape[0]
    heads, width = weight.shape[1], weight.shape[3]
    rows = 64
    return pl.pallas_call(
        project_kernel,
        grid=(2, CELLS // rows),
        in_specs=[
            pl.BlockSpec((groups, 4, rows, 2 * HEAD_DIM), lambda s, m: (0, 0, m, 0)),
            pl.BlockSpec((None, heads, HEAD_DIM, width), lambda s, m: (s, 0, 0, 0)),
            pl.BlockSpec((None, 4, rows, width), lambda s, m: (s, 0, m, 0)),
            pl.BlockSpec((None, 1, width), lambda s, m: (s, 0, 0)),
        ],
        out_specs=pl.BlockSpec((None, rows, 4 * width), lambda s, m: (s, m, 0)),
        out_shape=jax.ShapeDtypeStruct((2, CELLS, 4 * width), jnp.bfloat16),
        compiler_params=pltpu.CompilerParams(vmem_limit_bytes=40 * 2**20),
        name="project_merge",
    )(attended, weight, tokens, scale)


def place_kernel(row_ref, which_ref, valid_ref, first_ref, second_ref, out_ref):
    slot = pl.program_id(0)
    valid = valid_ref[slot] == 1
    first = jnp.logical_and(valid, which_ref[slot] == 0)
    second = jnp.logical_and(valid, which_ref[slot] == 1)

    @pl.when(first)
    def _():
        out_ref[...] = first_ref[...]

    @pl.when(second)
    def _():
        out_ref[...] = second_ref[...]

    @pl.when(jnp.logical_not(valid))
    def _():
        out_ref[...] = jnp.zeros_like(out_ref)


def place_tiles(first, second, row, which, valid):
    _, cells, columns = first.shape
    block = (None, cells, columns)
    return pl.pallas_call(
        place_kernel,
        grid_spec=pltpu.PrefetchScalarGridSpec(
            num_scalar_prefetch=3,
            grid=(CAP,),
            in_specs=[
                pl.BlockSpec(block, lambda k, r, w, v: (r[k], 0, 0)),
                pl.BlockSpec(block, lambda k, r, w, v: (r[k], 0, 0)),
            ],
            out_specs=pl.BlockSpec(block, lambda k, r, w, v: (k, 0, 0)),
        ),
        out_shape=jax.ShapeDtypeStruct((CAP, cells, columns), jnp.bfloat16),
        name="place_tiles",
    )(row, which, valid, first, second)


def slot_choice(tile_counts, owners, target):
    slot_index = jnp.arange(SLOTS, dtype=jnp.int32)[None, :]
    first_count = tile_counts[:, 0:1]
    holder = jnp.where(slot_index < first_count, owners[:, 0:1], owners[:, 1:2])
    living = slot_index < first_count + tile_counts[:, 1:2]
    owned = jnp.logical_and(living, holder == target).reshape(-1).astype(jnp.int32)
    order = jnp.arange(owned.shape[0], dtype=jnp.int32)
    before = jnp.sum(jnp.where(order[None, :] < order[:, None], owned[None, :], 0), axis=1)
    chosen = jnp.logical_and(
        before[None, :] == jnp.arange(CAP, dtype=jnp.int32)[:, None], owned[None, :] == 1
    )
    tile = jnp.sum(jnp.where(chosen, order[None, :], 0), axis=1)
    return tile // SLOTS, tile % SLOTS, jnp.any(chosen, axis=1).astype(jnp.int32)


def body(tokens, norm_gain, qkv_weight, qk_gain, out_weight, layer_scale, tile_counts, owners):
    own_rows = tokens[0]
    width_all = own_rows.shape[1]
    devices = lax.axis_size("dp")
    group = devices // 2
    position = lax.axis_index("dp")
    lower = position < group
    inner = position % group
    pairs = [list(range(group)), list(range(group, devices))]
    across = [(j, (j + group) % devices) for j in range(devices)]
    upward = [(j, j + group) for j in range(group)]

    gathered = lax.all_gather(own_rows, "dp", axis=0, tiled=True, axis_index_groups=pairs)
    other_block = lax.ppermute(qkv_weight, "dp", across)
    other_gain = lax.ppermute(qk_gain, "dp", across)
    own_weight = lax.all_gather(qkv_weight, "fsdp", axis=0, tiled=True)
    other_weight = lax.all_gather(other_block, "fsdp", axis=0, tiled=True)
    length = gathered.shape[0]
    spill = length - TILE

    def tile_of(values, spilled):
        moved = jnp.concatenate([spilled, values[: TILE - spill]], axis=0)
        return jnp.where(lower, values[:TILE], moved)

    values = gathered.astype(jnp.float32)
    normed = (
        values * lax.rsqrt(jnp.mean(values * values, axis=-1, keepdims=True) + EPSILON) * norm_gain
    ).astype(jnp.bfloat16)
    projected = [
        jnp.dot(normed, weight, preferred_element_type=jnp.float32)
        for weight in (own_weight, other_weight)
    ]
    queries = [part[:, :HEAD_DIM] for part in projected]
    keys = [part[:, HEAD_DIM : 2 * HEAD_DIM] for part in projected]
    vals = [part[:, 2 * HEAD_DIM :].astype(jnp.bfloat16) for part in projected]
    sums = jnp.stack(
        [
            sum(jnp.sum(q * q, axis=-1) for q in queries),
            sum(jnp.sum(k * k, axis=-1) for k in keys),
        ]
    )
    step = 1
    while step < group:
        swap = [(j, j ^ step) for j in range(devices)]
        sums = sums + lax.ppermute(sums, "dp", swap)
        step *= 2
    window = devices * HEAD_DIM
    factors = lax.rsqrt(sums / window + EPSILON)
    gains = (qk_gain, other_gain)
    queries = [
        (q * factors[0][:, None] * g[0]).astype(jnp.bfloat16) for q, g in zip(queries, gains)
    ]
    keys = [(k * factors[1][:, None] * g[1]).astype(jnp.bfloat16) for k, g in zip(keys, gains)]
    parts = [queries[0], queries[1], keys[0], keys[1], vals[0], vals[1]]
    swapped = [queries[1], queries[0], keys[1], keys[0], vals[1], vals[0]]
    spilled = lax.ppermute(
        jnp.concatenate([part[TILE:] for part in swapped], axis=1), "dp", upward
    )
    tiles = [
        tile_of(part, spilled[:, n * HEAD_DIM : (n + 1) * HEAD_DIM])
        for n, part in enumerate(parts)
    ]
    query = jnp.stack([patch_order(tiles[0][1:]), patch_order(tiles[1][1:])])
    key = jnp.stack(tiles[2:4])
    value = jnp.stack(tiles[4:6])
    factor = HEAD_DIM ** (-0.5)
    scores = jnp.einsum("sqc,skc->sqk", query, key, preferred_element_type=jnp.float32) * factor
    highest = jnp.max(scores, axis=-1, keepdims=True)
    exponent = jnp.exp(scores - highest)
    weights = (exponent / jnp.sum(exponent, axis=-1, keepdims=True)).astype(jnp.bfloat16)
    attended = jnp.einsum(
        "sqk,skc->sqc", weights, value, preferred_element_type=jnp.float32
    ).astype(jnp.bfloat16)
    both = jnp.where(
        lower,
        jnp.concatenate([attended[0], attended[1]], axis=1),
        jnp.concatenate([attended[1], attended[0]], axis=1),
    )
    heads_here = lax.all_gather(both, "dp", axis=0, axis_index_groups=pairs)
    heads_here = heads_here.reshape(group, 4, CELLS, 2 * HEAD_DIM)

    portion = width_all // group
    half_width = portion // 2
    weight_rows = lax.all_gather(out_weight, "dp", axis=0, tiled=True)
    if lax.axis_size("fsdp") == group:
        weight_full = lax.all_gather(weight_rows, "fsdp", axis=0)
        weight_here = lax.dynamic_index_in_dim(weight_full, inner, 0, keepdims=False)
    else:
        weight_full = lax.all_gather(weight_rows, "fsdp", axis=1, tiled=True)
        weight_here = lax.dynamic_slice_in_dim(weight_full, inner * portion, portion, 1)
    weight_here = weight_here.reshape(devices, HEAD_DIM, 2, half_width).transpose(2, 0, 1, 3)
    token_part = lax.dynamic_slice_in_dim(gathered, inner * portion, portion, 1)
    token_spill = lax.ppermute(token_part[TILE:], "dp", upward)
    token_tile = patch_order(tile_of(token_part, token_spill)[1:])
    token_tile = token_tile.reshape(4, CELLS, 2, half_width).transpose(2, 0, 1, 3)
    scale_here = lax.dynamic_slice_in_dim(layer_scale, inner * portion, portion, 0)
    merged = project_merge(heads_here, weight_here, token_tile, scale_here.reshape(2, 1, half_width))

    part_index = jnp.where(lower, 0, 1)
    first_out = lax.dynamic_index_in_dim(merged, part_index, 0, keepdims=False)
    second_out = lax.dynamic_index_in_dim(merged, 1 - part_index, 0, keepdims=False)
    straight = [(j, 2 * j) for j in range(group)] + [(group + j, 2 * j + 1) for j in range(group)]
    crossed = [(j, 2 * j + 1) for j in range(group)] + [(group + j, 2 * j) for j in range(group)]
    first_all = lax.all_gather(lax.ppermute(first_out, "dp", straight), "fsdp", axis=0)
    second_all = lax.all_gather(lax.ppermute(second_out, "dp", crossed), "fsdp", axis=0)
    row, slot, valid = slot_choice(tile_counts, owners, lax.axis_index("fsdp"))
    which = slot ^ (position % 2)
    return place_tiles(first_all, second_all, row, which, valid)


def solution(mesh):
    placed = (
        P("fsdp", "dp", None),
        P(),
        P("fsdp", "dp"),
        P(None, "dp"),
        P("dp", "fsdp"),
        P(),
        P(),
        P(),
    )
    return jax.shard_map(
        body, mesh=mesh, in_specs=placed, out_specs=P("fsdp", None, "dp"), check_vma=False
    )
```

time: 560 us -> 469 us (0.84); the launches traced: 553 us -> 468 us
  waiting for transfers between devices: 318 us -> 274 us
  blocking collectives: 29.2 us -> 0 us
  starting transfers between devices: 14.2 us -> 38.3 us
  local copies, waits for them, and re-layouts: 118 us -> 95.3 us
  matrix products: 35.7 us -> 21.1 us
  Pallas kernels: 0 us -> 14.3 us
  other arithmetic: 24.8 us -> 11 us
    all_to_all x3 -> x0, waiting for transfers between devices: 123 us -> none  [the longest x1 72.4 us: body(): lax.all_to_all(outgoing, 'fsdp', split_axis=0, concat_axis=0, tiled=True)]
    ppermute x0 -> x8, waiting for transfers between devices: none -> 65.1 us  [the longest x1 40.4 us: body(): other_block = lax.ppermute(qkv_weight, 'dp', across)]
    all_gather x3 -> x7, waiting for transfers between devices: 163 us -> 206 us  [the longest x1 60.9 us: body(): lax.all_gather(own_rows, 'dp', axis=0, tiled=True, axis_index_groups=pairs)]
    ppermute x0 -> x8, starting transfers between devices: none -> 38 us  [the longest x1 21.9 us: body(): lax.ppermute(second_out, 'dp', crossed)]
    all_gather x1, waiting for transfers between devices: 30.5 us -> 0.02 us  [body(): weight_rows = lax.all_gather(out_weight, 'dp', axis=0, tiled=True)]
    psum x1 -> x0, blocking collectives: 29.2 us -> none  [body(): lax.psum((jnp.sum(queries * queries, axis=-1), jnp.sum(keys_part * keys_p...]
    dynamic_slice x0 -> x5, local copies, waits for them, and re-layouts: none -> 28.2 us  [the longest x1 26.2 us: body(): lax.dynamic_index_in_dim(weight_full, inner, 0, keepdims=False)]
    transpose x2 -> x3, local copies, waits for them, and re-layouts: 24.5 us -> 1.53 us  [patch_order(): square = values.reshape(HALF, 2, HALF, 2, columns).transpose(1, 3, 0, 2, 4)]
  transfers between devices with their start and end apart: 7 -> 16, of which waited for: 6 -> 11; matrix products, arithmetic and copies ran while one was open for 9% -> 24% of each run, Pallas kernels for 0% -> 0%
where the time goes in v1:
time: 469 us; the launch traced here: 468 us
  waiting for transfers between devices  274 us (58%)
  local copies, waits for them, and re-layouts  95.3 us (20%)
  starting transfers between devices  38.3 us (8%)
  matrix products  21.1 us (4%)
  Pallas kernels  14.3 us (3%)
  between operations  14 us (3%)
  other arithmetic  11 us (2%)
    all_gather x1, waiting for transfers between devices, body(): lax.all_gather(own_rows, 'dp', axis=0, tiled=True, axis_index_groups=pairs)  60.9 us
    all_gather x1, waiting for transfers between devices, body(): lax.all_gather(lax.ppermute(second_out, 'dp', crossed), 'fsdp', axis=0)  41.4 us
    ppermute x1, waiting for transfers between devices, body(): other_block = lax.ppermute(qkv_weight, 'dp', across)  40.4 us
    all_gather x1, waiting for transfers between devices, body(): other_weight = lax.all_gather(other_block, 'fsdp', axis=0, tiled=True)  36.7 us
    all_gather x1, waiting for transfers between devices, body(): own_weight = lax.all_gather(qkv_weight, 'fsdp', axis=0, tiled=True)  33.1 us
    dynamic_slice x1, local copies, waits for them, and re-layouts, body(): lax.dynamic_index_in_dim(weight_full, inner, 0, keepdims=False)  26.2 us
    ppermute x1, starting transfers between devices, body(): lax.ppermute(second_out, 'dp', crossed)  21.9 us
    all_gather x1, waiting for transfers between devices, body(): lax.all_gather(lax.ppermute(first_out, 'dp', straight), 'fsdp', axis=0)  21.5 us
  transfers between devices with their start and end apart: 16, of which 11 were waited for; matrix products, arithmetic and copies ran while one was open for 24% of the time, Pallas kernels for 0%

profile of v1, /device:TPU:0, one launch (start us, length us, event | category | flops | bytes accessed | tf_op | source)
XLA Modules:
  0.0 467.9 jit_solution(10353828279517631672)
XLA Ops:
  6.5 0.7 all-gather.19.cloned.1.call-update
  8.1 4.1 collective-permute-start
  12.2 40.4 %collective-permute-done = bf16[800,384]{1,0:T(8,128)(2,1)S(1)} collective-permute-done((bf16[800,384]{1,0:T(8,128)(2,1)}, bf16[800,384]{1,0:T(8,128)(2,1)S(1)}, u32[]{:S(2)}, u32[]{:S(2)}) %collective-permute-start) | collective-permute-done | bytes 614432 | tf_op jit(solution)/shard_map/ppermute | solution.py:141
  52.6 0.8 copy-done.4
  54.8 60.9 %all-gather.21.cloned.1.call-done = bf16[1,1056,3200]{2,1,0:T(8,128)(2,1)} async-done(((bf16[1,264,3200]{2,1,0:T(8,128)(2,1)}), bf16[1,1056,3200]{2,1,0:T(8,128)(2,1)}) %all-gather.21.cloned.1.call-update) | async-done | bytes 6758416 | tf_op jit(solution)/shard_map/all_gather | solution.py:140
  115.7 4.3 fusion.1
  120.0 36.7 %all-gather.15.cloned.1.call-done = bf16[3200,384]{1,0:T(8,128)(2,1)} async-done(((bf16[800,384]{1,0:T(8,128)(2,1)}), bf16[3200,384]{1,0:T(8,128)(2,1)}) %all-gather.15.cloned.1.call-update) | async-done | bytes 2457616 | tf_op jit(solution)/shard_map/all_gather | solution.py:144
  156.7 7.0 %fusion.45 = (bf16[1056,384]{1,0:T(8,128)(2,1)S(1)}, f32[1056,384]{1,0:T(8,128)S(1)}) fusion(bf16[3200,384]{1,0:T(8,128)(2,1)} %all-gather.15.cloned.1.call-done, bf16[1,1056,3200]{2,1,0:T(8,128)(2,1)} %all-gather.21.cloned.1.call-done, f32[3200]{0:T(1024)S(1)} %copy-done.9, f32[1056]{0:T(1024)S(1)} %add_rsqrt_fusion.1), kind=kOutput, calls=%fused_computation.99 | convolution fusion | flops 2609147904 | bytes 11666048 | tf_op jit(solution)/shard_map/dot_general | solution.py:157
  163.7 33.1 %all-gather.13.cloned.1.call-done = bf16[3200,384]{1,0:T(8,128)(2,1)} async-done(((bf16[800,384]{1,0:T(8,128)(2,1)}), bf16[3200,384]{1,0:T(8,128)(2,1)}) %all-gather.13.cloned.1.call-update) | async-done | bytes 2457616 | tf_op jit(solution)/shard_map/all_gather | solution.py:143
  196.7 7.0 %fusion.46 = (bf16[1056,384]{1,0:T(8,128)(2,1)S(1)}, f32[1056,384]{1,0:T(8,128)S(1)}) fusion(bf16[3200,384]{1,0:T(8,128)(2,1)} %all-gather.13.cloned.1.call-done, bf16[1,1056,3200]{2,1,0:T(8,128)(2,1)} %all-gather.21.cloned.1.call-done, f32[3200]{0:T(1024)S(1)} %copy-done.9, f32[1056]{0:T(1024)S(1)} %add_rsqrt_fusion.1), kind=kOutput, calls=%fused_computation.100 | convolution fusion | flops 2609147904 | bytes 11666048 | tf_op jit(solution)/shard_map/dot_general | solution.py:157
  204.6 1.1 collective-permute-done.1
  205.7 1.6 collective-permute-start.2
  207.3 2.2 collective-permute-done.2
  213.5 4.5 collective-permute-start.4
  218.0 1.0 slice.229
  220.5 3.0 exponential_reduce_fusion
  223.6 1.1 fusion.23
  224.7 4.2 fusion.12
  229.1 1.0 copy.45
  230.2 0.8 dynamic_slice.19
  231.1 0.9 dynamic-slice_bitcast_fusion.2
  232.0 5.1 %collective-permute-start.5 = (bf16[31,800]{1,0:T(8,128)(2,1)S(1)}, bf16[31,800]{1,0:T(8,128)(2,1)S(1)}, u32[]{:S(2)}, u32[]{:S(2)}) collective-permute-start(bf16[31,800]{1,0:T(8,128)(2,1)S(1)} %dynamic-slice_bitcast_fusion.2), channel_id=1, source_target_pairs={{0,4},{1,5},{2,6},{3,7},{8,12},{9,13},{10,14},{11,15},{16,20},{17,... | collective-permute-start | bytes 148808 | tf_op jit(solution)/shard_map/ppermute | solution.py:220
  237.1 2.5 dynamic-slice_bitcast_fusion
  239.6 2.4 dynamic-slice_bitcast_fusion.1
  242.0 2.2 slice_select_fusion
  244.2 3.9 reshape.171
  248.1 1.5 copy.48
  249.5 6.9 %reshape_reshape.3 = bf16[4,256,2,400]{3,2,1,0:T(2,128)(2,1)S(1)} reshape(bf16[2,2,16,16,800]{4,3,2,1,0:T(8,128)(2,1)} %copy.48) | data formatting | bytes 3276800 | tf_op jit(solution)/shard_map/reshape;reshape | solution.py:222
  256.4 1.7 copy.58
  258.1 12.7 %all-gather.23.cloned.1.call-done = bf16[4096,800]{0,1:T(8,128)(2,1)} async-done(((bf16[1024,800]{0,1:T(8,128)(2,1)}), bf16[4096,800]{0,1:T(8,128)(2,1)}) %all-gather.23.cloned.1.call-update) | async-done | bytes 6553616 | tf_op jit(solution)/shard_map/all_gather | solution.py:213
  270.8 14.5 %reshape.175 = bf16[4,1024,800]{1,0,2:T(4,128)(2,1)} reshape(bf16[4096,800]{0,1:T(8,128)(2,1)} %all-gather.23.cloned.1.call-done) | data formatting | bytes 13107200 | tf_op jit(solution)/shard_map/all_gather | solution.py:213
  285.3 26.2 %dynamic-slice_reduce_fusion = bf16[1024,800]{0,1:T(8,128)(2,1)S(1)} fusion(bf16[4,1024,800]{1,0,2:T(4,128)(2,1)} %reshape.175, s32[]{:T(128)S(6)} %select_n.127), kind=kLoop, calls=%fused_computation.13 | loop fusion | bytes 3276804 | tf_op jit(solution)/shard_map/jit(dynamic_index_in_dim)/dynamic_slice | solution.py:214
  311.4 1.7 copy.56
  313.1 3.0 copy.47
  316.1 1.6 copy-done
  317.7 1.6 copy-done.1
  319.3 9.9 %project_merge.1 = bf16[2,256,1600]{2,1,0:T(8,128)(2,1)S(1)} custom-call(bf16[4,4,256,256]{3,2,1,0:T(8,128)(2,1)S(1)} %bitcast.71, bf16[2,8,128,400]{3,2,1,0:T(8,128)(2,1)S(1)} %bitcast.69, bf16[2,4,256,400]{3,2,1,0:T(8,128)(2,1)S(1)} %bitcast.70, f32[2,1,400]{2,1,0:T(1,128)S(1)} %reshape.172.scale_ref), custom_call_target="tpu_custom_call" | custom-call | tf_op jit(solution)/shard_map/project_merge/pallas_call | solution.py:59
  330.0 0.7 collective-permute-start.6
  330.7 0.9 copy-done.2
  332.3 21.9 %collective-permute-start.7 = (bf16[256,1600]{0,1:T(8,128)(2,1)S(1)}, bf16[256,1600]{0,1:T(8,128)(2,1)S(1)}, u32[]{:S(2)}, u32[]{:S(2)}) collective-permute-start(bf16[256,1600]{0,1:T(8,128)(2,1)S(1)} %bitcast.80), channel_id=1, source_target_pairs={{0,1},{1,3},{2,5},{3,7},{4,0},{5,2},{6,4},{7,6},{8,9},{9,11},{10,1... | collective-permute-start | bytes 2457608 | tf_op jit(solution)/shard_map/ppermute | solution.py:232
  354.2 20.6 %collective-permute-done.7 = bf16[256,1600]{0,1:T(8,128)(2,1)S(1)} collective-permute-done((bf16[256,1600]{0,1:T(8,128)(2,1)S(1)}, bf16[256,1600]{0,1:T(8,128)(2,1)S(1)}, u32[]{:S(2)}, u32[]{:S(2)}) %collective-permute-start.7) | collective-permute-done | bytes 819232 | tf_op jit(solution)/shard_map/ppermute | solution.py:232
  374.8 0.9 copy-done.3
  377.5 21.5 %all-gather.25.cloned.1.call-done = bf16[1024,1600]{0,1:T(8,128)(2,1)} async-done(((bf16[256,1600]{0,1:T(8,128)(2,1)}), bf16[1024,1600]{0,1:T(8,128)(2,1)}) %all-gather.25.cloned.1.call-update) | async-done | bytes 3276816 | tf_op jit(solution)/shard_map/all_gather | solution.py:231
  399.0 5.4 %copy.51 = bf16[1024,1600]{1,0:T(8,128)(2,1)} copy(bf16[1024,1600]{0,1:T(8,128)(2,1)} %all-gather.25.cloned.1.call-done) | data formatting | bytes 6553600 | tf_op jit(solution)/shard_map/all_gather | solution.py:231
  404.4 41.4 %all-gather.27.cloned.1.call-done = bf16[1024,1600]{0,1:T(8,128)(2,1)} async-done(((bf16[256,1600]{0,1:T(8,128)(2,1)}), bf16[1024,1600]{0,1:T(8,128)(2,1)}) %all-gather.27.cloned.1.call-update) | async-done | bytes 3276816 | tf_op jit(solution)/shard_map/all_gather | solution.py:232
  445.8 5.4 %copy.53 = bf16[1024,1600]{1,0:T(8,128)(2,1)} copy(bf16[1024,1600]{0,1:T(8,128)(2,1)} %all-gather.27.cloned.1.call-done) | data formatting | bytes 6553600 | tf_op jit(solution)/shard_map/all_gather | solution.py:232
  451.2 4.4 place_tiles.1
  455.6 5.5 %copy.54 = bf16[4,256,1600]{1,2,0:T(8,128)(2,1)} copy(bf16[4,256,1600]{2,1,0:T(8,128)(2,1)} %place_tiles.1) | data formatting | bytes 6553600 | tf_op jit(solution)/shard_map/place_tiles/pallas_call | solution.py:97
  (87 shorter events, 11.9 us)
Async XLA Ops:
  6.5 48.1 %copy-start.6 = (f32[2,128]{1,0:T(2,128)S(1)}, f32[2,128]{1,0:T(2,128)}, u32[]{:S(2)}) copy-start(f32[2,128]{1,0:T(2,128)} %param.11) | copy-start | bytes 3076
  6.5 47.5 %all-gather.19.cloned.1.call-start = ((), (), s32[]{:S(2)}) async-start(), calls=%async_computation.3 | async-start | bytes 1843200 | tf_op jit(solution)/shard_map/all_gather | solution.py:211
  7.3 108.4 %all-gather.21.cloned.1.call-start = ((), (), s32[]{:S(2)}) async-start(), calls=%async_computation.4 | async-start | bytes 8448000 | tf_op jit(solution)/shard_map/all_gather | solution.py:140
  8.0 148.7 %all-gather.15.cloned.1.call-start = ((), (), s32[]{:S(2)}) async-start(), calls=%async_computation.1 | async-start | bytes 3072000 | tf_op jit(solution)/shard_map/all_gather | solution.py:144
  8.1 44.5 %collective-permute-start = (bf16[800,384]{1,0:T(8,128)(2,1)}, bf16[800,384]{1,0:T(8,128)(2,1)S(1)}, u32[]{:S(2)}, u32[]{:S(2)}) collective-permute-start(bf16[800,384]{1,0:T(8,128)(2,1)} %param.10), channel_id=1, source_target_pairs={{0,4},{1,5},{2,6},{3,7},{4,0},{5,1},{6,2},{7,3},{8,12},{9,13},{10,... | collective-permute-start | bytes 1843208 | tf_op jit(solution)/shard_map/ppermute | solution.py:141
  52.6 0.8 copy-start.4
  53.4 143.3 %all-gather.13.cloned.1.call-start = ((), (), s32[]{:S(2)}) async-start(), calls=%async_computation | async-start | bytes 3072000 | tf_op jit(solution)/shard_map/all_gather | solution.py:143
  54.0 216.8 %all-gather.23.cloned.1.call-start = ((), (), s32[]{:S(2)}) async-start(), calls=%async_computation.5 | async-start | bytes 8192000 | tf_op jit(solution)/shard_map/all_gather | solution.py:213
  54.6 102.1 %copy-start.9 = (f32[3200]{0:T(1024)S(1)}, f32[3200]{0:T(1024)}, u32[]{:S(2)}) copy-start(f32[3200]{0:T(1024)} %param.9) | copy-start | bytes 38404
  54.6 261.5 %all-gather.17.cloned.1.call-start = ((), (), s32[]{:S(2)}) async-start(), calls=%async_computation.2 | async-start | bytes 2621440 | tf_op jit(solution)/shard_map/all_gather | solution.py:206
  54.7 152.6 %collective-permute-start.3 = (f32[2,128]{1,0:T(2,128)S(1)}, f32[2,128]{1,0:T(2,128)S(1)}, u32[]{:S(2)}, u32[]{:S(2)}) collective-permute-start(f32[2,128]{1,0:T(2,128)S(1)} %copy-done.6), channel_id=1, source_target_pairs={{0,4},{1,5},{2,6},{3,7},{4,0},{5,1},{6,2},{7,3},{8,12},{9,13},{10,... | collective-permute-start | bytes 3080 | tf_op jit(solution)/shard_map/ppermute | solution.py:142
  203.7 9.2 %copy-start.5 = (bf16[1056,384]{1,0:T(8,128)(2,1)}, bf16[1056,384]{1,0:T(8,128)(2,1)S(1)}, u32[]{:S(2)}) copy-start(bf16[1056,384]{1,0:T(8,128)(2,1)S(1)} %get-tuple-element.39) | copy-start | bytes 2433028
  204.5 1.2 collective-permute-start.1
  205.7 3.7 collective-permute-start.2
  213.5 6.4 %collective-permute-start.4 = (bf16[31,768]{1,0:T(8,128)(2,1)}, bf16[31,768]{1,0:T(8,128)(2,1)S(1)}, u32[]{:S(2)}, u32[]{:S(2)}) collective-permute-start(bf16[31,768]{1,0:T(8,128)(2,1)} %constant_dynamic-update-slice_fusion), channel_id=1, source_target_pairs={{0,4},{1,5},{2,6},{3,7},{8,12},{9,13},{10,14},{11,15},{16,20},{17,... | collective-permute-start | bytes 142856 | tf_op jit(solution)/shard_map/ppermute | solution.py:183
  230.1 168.9 %all-gather.25.cloned.1.call-start = ((), (), s32[]{:S(2)}) async-start(), calls=%async_computation.6 | async-start | bytes 4096000 | tf_op jit(solution)/shard_map/all_gather | solution.py:231
  232.0 10.0 %collective-permute-start.5 = (bf16[31,800]{1,0:T(8,128)(2,1)S(1)}, bf16[31,800]{1,0:T(8,128)(2,1)S(1)}, u32[]{:S(2)}, u32[]{:S(2)}) collective-permute-start(bf16[31,800]{1,0:T(8,128)(2,1)S(1)} %dynamic-slice_bitcast_fusion.2), channel_id=1, source_target_pairs={{0,4},{1,5},{2,6},{3,7},{8,12},{9,13},{10,14},{11,15},{16,20},{17,... | collective-permute-start | bytes 148808 | tf_op jit(solution)/shard_map/ppermute | solution.py:220
  316.1 1.6 copy-start
  317.7 1.6 copy-start.1
  329.2 46.5 %copy-start.7 = (s32[4,2]{0,1:T(2,128)S(1)}, s32[4,2]{0,1:T(2,128)}, u32[]{:S(2)}) copy-start(s32[4,2]{0,1:T(2,128)} %param.15) | copy-start | bytes 100
  329.2 46.5 %copy-start.8 = (s32[4,2]{0,1:T(2,128)S(1)}, s32[4,2]{0,1:T(2,128)}, u32[]{:S(2)}) copy-start(s32[4,2]{0,1:T(2,128)} %param.14) | copy-start | bytes 100
  330.0 0.7 collective-permute-start.6
  330.7 0.9 copy-start.2
  331.6 114.2 %all-gather.27.cloned.1.call-start = ((), (), s32[]{:S(2)}) async-start(), calls=%async_computation.7 | async-start | bytes 4096000 | tf_op jit(solution)/shard_map/all_gather | solution.py:232
  332.3 42.5 %collective-permute-start.7 = (bf16[256,1600]{0,1:T(8,128)(2,1)S(1)}, bf16[256,1600]{0,1:T(8,128)(2,1)S(1)}, u32[]{:S(2)}, u32[]{:S(2)}) collective-permute-start(bf16[256,1600]{0,1:T(8,128)(2,1)S(1)} %bitcast.80), channel_id=1, source_target_pairs={{0,1},{1,3},{2,5},{3,7},{4,0},{5,2},{6,4},{7,6},{8,9},{9,11},{10,1... | collective-permute-start | bytes 2457608 | tf_op jit(solution)/shard_map/ppermute | solution.py:232
  374.8 0.9 copy-start.3
Sparse Core Ops, SparseCore 0:
  8.9 41.7 all-gather.18
  52.3 63.3 all-gather.20
  117.5 39.1 all-gather.14
  158.4 38.2 all-gather.12
  198.4 72.3 all-gather.22
  272.2 26.4 all-gather.16
  331.7 67.2 all-gather.24
  400.8 44.9 all-gather.26

commit v2 on v1

--- a/solution.py
+++ b/solution.py
@@ -1,3 +1,5 @@
+import functools
+
 import jax
 import jax.numpy as jnp
 from jax import lax
@@ -72,42 +74,287 @@
     )(attended, weight, tokens, scale)
 
 
-def place_kernel(row_ref, which_ref, valid_ref, first_ref, second_ref, out_ref):
-    slot = pl.program_id(0)
-    valid = valid_ref[slot] == 1
-    first = jnp.logical_and(valid, which_ref[slot] == 0)
-    second = jnp.logical_and(valid, which_ref[slot] == 1)
-
-    @pl.when(first)
+MESH = pl.DeviceIdType.MESH
+
+
+def gather_kernel(
+    fsdp_size, dp_size, rows_ref, qkv_ref, proj_ref, tokens_out, qkv_out, proj_out,
+    local_sem, row_send, row_recv, qkv_send, qkv_recv, proj_send, proj_recv,
+):
+    mine, position = lax.axis_index("fsdp"), lax.axis_index("dp")
+    group = dp_size // 2
+    half = position // group
+    inner = position - half * group
+    base = half * group
+    partner = lax.rem(position + group, dp_size)
+    sibling = base + (inner + 1 - 2 * lax.rem(inner, 2))
+    chips = group // 2
+    near = [base + lax.rem(inner + 2 * r, group) for r in range(1, chips)]
+    across = [lax.rem(mine + r, fsdp_size) for r in range(1, fsdp_size)]
+
+    barrier = pltpu.get_barrier_semaphore()
+    fixed = [(mine, p) for p in near + [sibling, partner]] + [(f, position) for f in across]
+    for target in fixed:
+        pl.semaphore_signal(barrier, inc=1, device_id=target, device_id_type=MESH)
+    for source in range(dp_size):
+
+        @pl.when(jnp.logical_or(mine != inner, position != source))
+        def _():
+            pl.semaphore_signal(barrier, inc=1, device_id=(inner, source), device_id_type=MESH)
+
+    pl.semaphore_wait(barrier, len(fixed) + 2 * fsdp_size - jnp.where(mine == inner, 1, 0))
+
+    def send(src, dst, send_sem, recv_sem, target):
+        copy = pltpu.make_async_remote_copy(
+            src_ref=src, dst_ref=dst, send_sem=send_sem, recv_sem=recv_sem,
+            device_id=target, device_id_type=MESH,
+        )
+        copy.start()
+        return copy
+
+    def arrived(ref, sem):
+        pltpu.make_async_copy(ref, ref, sem).wait()
+
+    sent = []
+    sent.append(send(qkv_ref, qkv_out.at[1, mine], qkv_send.at[0], qkv_recv.at[1, mine], (mine, partner)))
+    for n, peer in enumerate(near):
+        sent.append(send(rows_ref, tokens_out.at[inner], row_send.at[n], row_recv.at[inner], (mine, peer)))
+    sent.append(
+        send(rows_ref, tokens_out.at[inner], row_send.at[chips], row_recv.at[inner], (mine, sibling))
+    )
+    for n, peer in enumerate(across):
+        sent.append(
+            send(qkv_ref, qkv_out.at[0, mine], qkv_send.at[1 + n], qkv_recv.at[0, mine], (peer, position))
+        )
+    own_rows = pltpu.make_async_copy(rows_ref, tokens_out.at[inner], local_sem.at[0])
+    own_qkv = pltpu.make_async_copy(qkv_ref, qkv_out.at[0, mine], local_sem.at[1])
+    own_rows.start()
+    own_qkv.start()
+
+    def proj_copy(row, side):
+        slot = row * 2 + side
+        return pltpu.make_async_remote_copy(
+            src_ref=proj_ref, dst_ref=proj_out.at[position], send_sem=proj_send.at[slot],
+            recv_sem=proj_recv.at[position], device_id=(row, side * group + mine), device_id_type=MESH,
+        )
+
+    own_proj = pltpu.make_async_copy(proj_ref, proj_out.at[position], local_sem.at[2])
+
+    def each_proj(action):
+        for row in range(fsdp_size):
+            for side in range(2):
+
+                @pl.when(jnp.logical_or(row != mine, side * group + mine != position))
+                def _():
+                    action(proj_copy(row, side))
+
+    each_proj(lambda copy: copy.start())
+
+    @pl.when(mine == inner)
     def _():
-        out_ref[...] = first_ref[...]
-
-    @pl.when(second)
+        own_proj.start()
+
+    arrived(qkv_out.at[1, mine], qkv_recv.at[1, mine])
+    for n, peer in enumerate(across):
+        sent.append(
+            send(qkv_out.at[1, mine], qkv_out.at[1, mine], qkv_send.at[fsdp_size + n],
+                 qkv_recv.at[1, mine], (peer, position))
+        )
+    for n in range(1, chips):
+        block = lax.rem(inner + 2 * (chips - n), group)
+        arrived(tokens_out.at[block], row_recv.at[block])
+        sent.append(
+            send(tokens_out.at[block], tokens_out.at[block], row_send.at[chips + n],
+                 row_recv.at[block], (mine, sibling))
+        )
+    other = inner + 1 - 2 * lax.rem(inner, 2)
+    for n in range(chips):
+        block = lax.rem(other + 2 * n, group)
+        arrived(tokens_out.at[block], row_recv.at[block])
+    for peer in across:
+        for kind in range(2):
+            arrived(qkv_out.at[kind, peer], qkv_recv.at[kind, peer])
+    for source in range(dp_size):
+
+        @pl.when(jnp.logical_or(mine != inner, position != source))
+        def _():
+            arrived(proj_out.at[source], proj_recv.at[source])
+
+    for copy in sent:
+        copy.wait_send()
+    each_proj(lambda copy: copy.wait_send())
+    own_rows.wait()
+    own_qkv.wait()
+
+    @pl.when(mine == inner)
     def _():
-        out_ref[...] = second_ref[...]
+        own_proj.wait()
+
+
+def gather_inputs(rows, qkv, proj):
+    fsdp_size, dp_size = lax.axis_size("fsdp"), lax.axis_size("dp")
+    group = dp_size // 2
+    anywhere = pl.BlockSpec(memory_space=pl.ANY)
+    dma = pltpu.SemaphoreType.DMA
+    return pl.pallas_call(
+        functools.partial(gather_kernel, fsdp_size, dp_size),
+        in_specs=[anywhere] * 3,
+        out_specs=[anywhere] * 3,
+        out_shape=[
+            jax.ShapeDtypeStruct((group,) + rows.shape, rows.dtype),
+            jax.ShapeDtypeStruct((2, fsdp_size) + qkv.shape, qkv.dtype),
+            jax.ShapeDtypeStruct((dp_size,) + proj.shape, proj.dtype),
+        ],
+        scratch_shapes=[
+            dma((3,)),
+            dma((group,)),
+            dma((group,)),
+            dma((2 * fsdp_size - 1,)),
+            dma((2, fsdp_size)),
+            dma((2 * fsdp_size,)),
+            dma((dp_size,)),
+        ],
+        compiler_params=pltpu.CompilerParams(collective_id=0, has_side_effects=True),
+        name="gather_inputs",
+    )(rows, qkv, proj)
+
+
+PIECES = 4
+
+
+def deliver_kernel(
+    fsdp_size, dp_size, merged_ref, out_ref, local_sem, first_send, first_recv, next_send, next_recv
+):
+    mine, position = lax.axis_index("fsdp"), lax.axis_index("dp")
+    group = dp_size // 2
+    half = position // group
+    inner = position - half * group
+    across = [lax.rem(mine + r, fsdp_size) for r in range(1, fsdp_size)]
+    size = merged_ref.shape[1] // PIECES
+    barrier = pltpu.get_barrier_semaphore()
+    for peer in across:
+        pl.semaphore_signal(barrier, inc=1, device_id=(peer, position), device_id_type=MESH)
+    origin = position // 2
+    for side in range(2):
+
+        @pl.when(side * group + origin != position)
+        def _():
+            pl.semaphore_signal(
+                barrier, inc=1, device_id=(mine, side * group + origin), device_id_type=MESH
+            )
+
+    pl.semaphore_wait(barrier, len(across) + 2 - jnp.where(origin == inner, 1, 0))
+
+    def first_copy(part, piece):
+        place = pl.ds(piece * size, size)
+        return pltpu.make_async_remote_copy(
+            src_ref=merged_ref.at[part, place], dst_ref=out_ref.at[mine, half, place],
+            send_sem=first_send.at[part, piece], recv_sem=first_recv.at[half, piece],
+            device_id=(mine, 2 * inner + part), device_id_type=MESH,
+        )
+
+    def own_copy(part, piece):
+        place = pl.ds(piece * size, size)
+        return pltpu.make_async_copy(
+            merged_ref.at[part, place], out_ref.at[mine, half, place], local_sem.at[piece]
+        )
+
+    for piece in range(PIECES):
+        for part in range(2):
+
+            @pl.when(2 * inner + part != position)
+            def _():
+                first_copy(part, piece).start()
+
+            @pl.when(2 * inner + part == position)
+            def _():
+                own_copy(part, piece).start()
+
+    sent = []
+    for piece in range(PIECES):
+        place = pl.ds(piece * size, size)
+        for side in range(2):
+            ref = out_ref.at[mine, side, place]
+            here = side * group + origin == position
+
+            @pl.when(jnp.logical_not(here))
+            def _():
+                pltpu.make_async_copy(ref, ref, first_recv.at[side, piece]).wait()
+
+            @pl.when(here)
+            def _():
+                pltpu.make_async_copy(ref, ref, local_sem.at[piece]).wait()
+
+            for n, peer in enumerate(across):
+                copy = pltpu.make_async_remote_copy(
+                    src_ref=ref, dst_ref=ref, send_sem=next_send.at[n, side, piece],
+                    recv_sem=next_recv.at[mine, side, piece],
+                    device_id=(peer, position), device_id_type=MESH,
+                )
+                copy.start()
+                sent.append(copy)
+    for piece in range(PIECES):
+        place = pl.ds(piece * size, size)
+        for side in range(2):
+            for peer in across:
+                ref = out_ref.at[peer, side, place]
+                pltpu.make_async_copy(ref, ref, next_recv.at[peer, side, piece]).wait()
+    for copy in sent:
+        copy.wait_send()
+    for piece in range(PIECES):
+        for part in range(2):
+
+            @pl.when(2 * inner + part != position)
+            def _():
+                first_copy(part, piece).wait_send()
+
+
+def deliver(merged):
+    fsdp_size, dp_size = lax.axis_size("fsdp"), lax.axis_size("dp")
+    dma = pltpu.SemaphoreType.DMA
+    return pl.pallas_call(
+        functools.partial(deliver_kernel, fsdp_size, dp_size),
+        in_specs=[pl.BlockSpec(memory_space=pl.ANY)],
+        out_specs=pl.BlockSpec(memory_space=pl.ANY),
+        out_shape=jax.ShapeDtypeStruct((fsdp_size,) + merged.shape, merged.dtype),
+        scratch_shapes=[
+            dma((PIECES,)),
+            dma((2, PIECES)),
+            dma((2, PIECES)),
+            dma((fsdp_size - 1, 2, PIECES)),
+            dma((fsdp_size, 2, PIECES)),
+        ],
+        compiler_params=pltpu.CompilerParams(collective_id=1, has_side_effects=True),
+        name="deliver",
+    )(merged)
+
+
+def place_kernel(tile_ref, valid_ref, all_ref, out_ref):
+    valid = valid_ref[pl.program_id(0)] == 1
+
+    @pl.when(valid)
+    def _():
+        out_ref[...] = all_ref[...]
 
     @pl.when(jnp.logical_not(valid))
     def _():
         out_ref[...] = jnp.zeros_like(out_ref)
 
 
-def place_tiles(first, second, row, which, valid):
-    _, cells, columns = first.shape
+def place_tiles(tiles, tile, valid):
+    _, cells, columns = tiles.shape
     block = (None, cells, columns)
     return pl.pallas_call(
         place_kernel,
         grid_spec=pltpu.PrefetchScalarGridSpec(
-            num_scalar_prefetch=3,
+            num_scalar_prefetch=2,
             grid=(CAP,),
-            in_specs=[
-                pl.BlockSpec(block, lambda k, r, w, v: (r[k], 0, 0)),
-                pl.BlockSpec(block, lambda k, r, w, v: (r[k], 0, 0)),
-            ],
-            out_specs=pl.BlockSpec(block, lambda k, r, w, v: (k, 0, 0)),
+            in_specs=[pl.BlockSpec(block, lambda k, t, v: (t[k], 0, 0))],
+            out_specs=pl.BlockSpec(block, lambda k, t, v: (k, 0, 0)),
         ),
         out_shape=jax.ShapeDtypeStruct((CAP, cells, columns), jnp.bfloat16),
         name="place_tiles",
-    )(row, which, valid, first, second)
+    )(tile, valid, tiles)
 
 
 def slot_choice(tile_counts, owners, target):
@@ -122,7 +369,7 @@
         before[None, :] == jnp.arange(CAP, dtype=jnp.int32)[:, None], owned[None, :] == 1
     )
     tile = jnp.sum(jnp.where(chosen, order[None, :], 0), axis=1)
-    return tile // SLOTS, tile % SLOTS, jnp.any(chosen, axis=1).astype(jnp.int32)
+    return tile, jnp.any(chosen, axis=1).astype(jnp.int32)
 
 
 def body(tokens, norm_gain, qkv_weight, qk_gain, out_weight, layer_scale, tile_counts, owners):
@@ -137,11 +384,13 @@
     across = [(j, (j + group) % devices) for j in range(devices)]
     upward = [(j, j + group) for j in range(group)]
 
-    gathered = lax.all_gather(own_rows, "dp", axis=0, tiled=True, axis_index_groups=pairs)
-    other_block = lax.ppermute(qkv_weight, "dp", across)
+    if lax.axis_size("fsdp") != group:
+        raise ValueError("mesh axes")
+    gathered, weights_qkv, weight_here = gather_inputs(own_rows, qkv_weight, out_weight)
+    gathered = gathered.reshape(-1, width_all)
+    weights_qkv = weights_qkv.reshape(2, width_all, -1)
+    own_weight, other_weight = weights_qkv[0], weights_qkv[1]
     other_gain = lax.ppermute(qk_gain, "dp", across)
-    own_weight = lax.all_gather(qkv_weight, "fsdp", axis=0, tiled=True)
-    other_weight = lax.all_gather(other_block, "fsdp", axis=0, tiled=True)
     length = gathered.shape[0]
     spill = length - TILE
 
@@ -208,13 +457,6 @@
 
     portion = width_all // group
     half_width = portion // 2
-    weight_rows = lax.all_gather(out_weight, "dp", axis=0, tiled=True)
-    if lax.axis_size("fsdp") == group:
-        weight_full = lax.all_gather(weight_rows, "fsdp", axis=0)
-        weight_here = lax.dynamic_index_in_dim(weight_full, inner, 0, keepdims=False)
-    else:
-        weight_full = lax.all_gather(weight_rows, "fsdp", axis=1, tiled=True)
-        weight_here = lax.dynamic_slice_in_dim(weight_full, inner * portion, portion, 1)
     weight_here = weight_here.reshape(devices, HEAD_DIM, 2, half_width).transpose(2, 0, 1, 3)
     token_part = lax.dynamic_slice_in_dim(gathered, inner * portion, portion, 1)
     token_spill = lax.ppermute(token_part[TILE:], "dp", upward)
@@ -223,16 +465,9 @@
     scale_here = lax.dynamic_slice_in_dim(layer_scale, inner * portion, portion, 0)
     merged = project_merge(heads_here, weight_here, token_tile, scale_here.reshape(2, 1, half_width))
 
-    part_index = jnp.where(lower, 0, 1)
-    first_out = lax.dynamic_index_in_dim(merged, part_index, 0, keepdims=False)
-    second_out = lax.dynamic_index_in_dim(merged, 1 - part_index, 0, keepdims=False)
-    straight = [(j, 2 * j) for j in range(group)] + [(group + j, 2 * j + 1) for j in range(group)]
-    crossed = [(j, 2 * j + 1) for j in range(group)] + [(group + j, 2 * j) for j in range(group)]
-    first_all = lax.all_gather(lax.ppermute(first_out, "dp", straight), "fsdp", axis=0)
-    second_all = lax.all_gather(lax.ppermute(second_out, "dp", crossed), "fsdp", axis=0)
-    row, slot, valid = slot_choice(tile_counts, owners, lax.axis_index("fsdp"))
-    which = slot ^ (position % 2)
-    return place_tiles(first_all, second_all, row, which, valid)
+    delivered = deliver(merged)
+    tile, valid = slot_choice(tile_counts, owners, lax.axis_index("fsdp"))
+    return place_tiles(delivered.reshape((-1,) + delivered.shape[2:]), tile, valid)
 
 
 def solution(mesh):

time: 469 us -> 331 us (0.71)
  waiting for transfers between devices: 274 us -> 2.97 us
  Pallas kernels: 14.3 us -> 201 us
  local copies, waits for them, and re-layouts: 95.3 us -> 45.1 us
  starting transfers between devices: 38.3 us -> 30.1 us
  other arithmetic: 11 us -> 17.3 us
  matrix products: 21.1 us -> 16.3 us
    all_gather x7 -> x0, waiting for transfers between devices: 206 us -> none  [the longest x1 60.9 us: body(): lax.all_gather(own_rows, 'dp', axis=0, tiled=True, axis_index_groups=pairs)]
    pallas_call x0 -> x2, Pallas kernels: none -> 187 us  [the longest x1 102 us: gather_inputs(): pl.pallas_call(functools.partial(gather_kernel, fsdp_size, dp_size), in_s...]
    ppermute x3 -> x0, waiting for transfers between devices: 61 us -> none  [the longest x1 40.4 us: body(): other_block = lax.ppermute(qkv_weight, 'dp', across)]
    dynamic_slice x4 -> x0, local copies, waits for them, and re-layouts: 27.5 us -> none  [the longest x1 26.2 us: body(): lax.dynamic_index_in_dim(weight_full, inner, 0, keepdims=False)]
    ppermute x3 -> x0, starting transfers between devices: 26.8 us -> none  [the longest x1 21.9 us: body(): lax.ppermute(second_out, 'dp', crossed)]
    all_gather x3 -> x0, local copies, waits for them, and re-layouts: 25.3 us -> none  [the longest x1 14.5 us: body(): weight_full = lax.all_gather(weight_rows, 'fsdp', axis=0)]
    ppermute x1, starting transfers between devices: 0.07 us -> 12.3 us  [body(): other_gain = lax.ppermute(qk_gain, 'dp', across)]
    ppermute x2, starting transfers between devices: 1.62 us -> 8.48 us  [body(): sums = sums + lax.ppermute(sums, 'dp', swap)]
  transfers between devices with their start and end apart: 16 -> 6, of which waited for: 11 -> 2; matrix products, arithmetic and copies ran while one was open for 24% -> 11% of each run, Pallas kernels for 0% -> 0%
where the time goes in v2:
time: 331 us; the launch traced here: 326 us
  Pallas kernels  201 us (61%)
  local copies, waits for them, and re-layouts  45.1 us (14%)
  starting transfers between devices  30.1 us (9%)
  other arithmetic  17.3 us (5%)
  matrix products  16.3 us (5%)
  between operations  13.9 us (4%)
    pallas_call x1, Pallas kernels, gather_inputs(): pl.pallas_call(functools.partial(gather_kernel, fsdp_size, dp_size), in_s...  102 us
    pallas_call x1, Pallas kernels, deliver(): pl.pallas_call(functools.partial(deliver_kernel, fsdp_size, dp_size), in_...  84.6 us
    ppermute x1, starting transfers between devices, body(): other_gain = lax.ppermute(qk_gain, 'dp', across)  12.3 us
    another operation x2, local copies, waits for them, and re-layouts, body(): token_tile.reshape(4, CELLS, 2, half_width).transpose(2, 0, 1, 3)  10.9 us
    pallas_call x1, Pallas kernels, project_merge(): pl.pallas_call(project_kernel, grid=(2, CELLS // rows), in_specs=[pl.Bloc...  9.92 us
    dot_general x2, matrix products, body(): jnp.dot(normed, weight, preferred_element_type=jnp.float32)  9.17 us
    ppermute x2, starting transfers between devices, body(): sums = sums + lax.ppermute(sums, 'dp', swap)  8.48 us
    unnamed x32, local copies, waits for them, and re-layouts  7.04 us
  transfers between devices with their start and end apart: 6, of which 2 were waited for; matrix products, arithmetic and copies ran while one was open for 11% of the time, Pallas kernels for 0%

profile of v2, /device:TPU:0, one launch (start us, length us, event | category | flops | bytes accessed | tf_op | source)
XLA Modules:
  0.0 326.2 jit_solution(16995435299935822434)
XLA Ops:
  6.5 1.8 copy.32.proj_ref
  8.3 101.9 %gather_inputs.1 = (bf16[4,264,3200]{2,1,0:T(8,128)(2,1)}, bf16[2,4,800,384]{3,2,1,0:T(8,128)(2,1)}, bf16[8,128,800]{2,1,0:T(8,128)(2,1)}) custom-call(bf16[264,3200]{1,0:T(8,128)(2,1)} %bitcast.66, bf16[800,384]{1,0:T(8,128)(2,1)} %qkv_ref.1, bf16[128,800]{1,0:T(8,128)(2,1)} %copy.32.proj_ref), custom_call_target="tpu_custom_call" | custom-call | tf_op jit(solution)/shard_map/gather_inputs/pallas_call | solution.py:199
  110.3 4.5 %fusion.1 = f32[4,264]{1,0:T(4,128)S(1)} fusion(bf16[4,264,3200]{2,1,0:T(8,128)(2,1)} %get-tuple-element.8), kind=kLoop, calls=%fused_computation.3 | loop fusion | flops 10136544 | bytes 6762624 | tf_op jit(solution)/shard_map/reduce_sum | solution.py:403
  114.8 1.9 fusion.38
  116.7 0.8 slice-done.1
  117.5 2.5 fusion.3
  120.0 5.4 %fusion.42 = (bf16[1056,384]{1,0:T(8,128)(2,1)S(1)}, f32[1056,384]{1,0:T(8,128)S(1)}) fusion(bf16[1056,3200]{1,0:T(8,128)(2,1)S(1)} %bitcast.61, bf16[3200,384]{1,0:T(8,128)(2,1)} %bitcast.65), kind=kOutput, calls=%fused_computation.88 | convolution fusion | flops 2595631104 | bytes 11649024 | tf_op jit(solution)/shard_map/dot_general | solution.py:406
  125.5 3.7 %fusion.41 = (bf16[1056,384]{1,0:T(8,128)(2,1)S(1)}, f32[1056,384]{1,0:T(8,128)S(1)}) fusion(bf16[1056,3200]{1,0:T(8,128)(2,1)S(1)} %bitcast.62, bf16[3200,384]{1,0:T(8,128)(2,1)S(1)} %bitcast.64), kind=kOutput, calls=%fused_computation.87 | convolution fusion | flops 2595631104 | bytes 11649024 | tf_op jit(solution)/shard_map/dot_general | solution.py:406
  129.2 0.7 multiply_reduce_fusion.3
  130.1 12.3 %collective-permute-start.2 = (f32[2,128]{1,0:T(2,128)S(1)}, f32[2,128]{1,0:T(2,128)S(1)}, u32[]{:S(2)}, u32[]{:S(2)}) collective-permute-start(f32[2,128]{1,0:T(2,128)S(1)} %copy-done.8), channel_id=1, source_target_pairs={{0,4},{1,5},{2,6},{3,7},{4,0},{5,1},{6,2},{7,3},{8,12},{9,13},{10,... | collective-permute-start | bytes 3080 | tf_op jit(solution)/shard_map/ppermute | solution.py:393
  142.4 8.4 %collective-permute-start.1 = (f32[2,1056]{1,0:T(2,128)S(1)}, f32[2,1056]{1,0:T(2,128)S(1)}, u32[]{:S(2)}, u32[]{:S(2)}) collective-permute-start(f32[2,1056]{1,0:T(2,128)S(1)} %fusion.37), channel_id=1, source_target_pairs={{0,2},{1,3},{2,0},{3,1},{4,6},{5,7},{6,4},{7,5},{8,10},{9,11},{10,... | collective-permute-start | bytes 25352 | tf_op jit(solution)/shard_map/ppermute | solution.py:421
  150.8 1.6 collective-permute-done.1
  152.5 0.4 multiply_convert_fusion.2
  152.9 3.9 %collective-permute-start.3 = (bf16[31,768]{1,0:T(8,128)(2,1)S(1)}, bf16[31,768]{1,0:T(8,128)(2,1)S(1)}, u32[]{:S(2)}, u32[]{:S(2)}) collective-permute-start(bf16[31,768]{1,0:T(8,128)(2,1)S(1)} %constant_dynamic-update-slice_fusion), channel_id=1, source_target_pairs={{0,4},{1,5},{2,6},{3,7},{8,12},{9,13},{10,14},{11,15},{16,20},{17,... | collective-permute-start | bytes 142856 | tf_op jit(solution)/shard_map/ppermute | solution.py:432
  157.1 1.3 collective-permute-done.3
  158.4 0.2 slice_select_fusion.5
  158.6 0.2 slice_select_fusion.4
  158.9 1.1 fusion.19
  159.9 1.1 fusion.18
  161.0 0.1 fusion.21
  161.1 0.1 fusion.20
  161.2 3.0 exponential_reduce_fusion
  164.3 4.1 %fusion.8 = bf16[2,1024,128]{1,2,0:T(8,128)(2,1)S(1)} fusion(f32[2,1024]{1,0:T(2,128)S(1)} %exponential_reduce_fusion, bf16[1,1025,128]{2,1,0:T(8,128)(2,1)S(1)} %fusion.18, bf16[1,1025,128]{2,1,0:T(8,128)(2,1)S(1)} %fusion.19, bf16[1,1025,128]{2,1,0:T(8,128)(2,1)S(1)} %fusion.20, bf16[1,1025,128]{2,1,0:T(8,128)(2,1)S(1)} %fusion.21, ...), kind=kOutput, calls=%fused_computation.16 | convolution fusion | flops 1084239360 | bytes 2106368 | tf_op jit(solution)/shard_map/sqk,skc->sqc/dot_general | solution.py:447
  168.5 0.1 maximum_select_fusion
  168.6 1.0 copy.35
  169.7 0.9 dynamic-slice.1
  170.6 5.4 %collective-permute-start.4 = (bf16[31,800]{1,0:T(8,128)(2,1)S(1)}, bf16[31,800]{1,0:T(8,128)(2,1)S(1)}, u32[]{:S(2)}, u32[]{:S(2)}) collective-permute-start(bf16[31,800]{1,0:T(8,128)(2,1)S(1)} %dynamic-slice.1), channel_id=1, source_target_pairs={{0,4},{1,5},{2,6},{3,7},{8,12},{9,13},{10,14},{11,15},{16,20},{17,... | collective-permute-start | bytes 148808 | tf_op jit(solution)/shard_map/ppermute | solution.py:462
  176.1 0.1 reshape.209
  176.2 0.1 select_reduce_fusion
  176.4 0.7 select_reduce_fusion.1.tile_ref
  177.0 3.6 %constant_dynamic-slice_fusion = bf16[994,800]{1,0:T(8,128)(2,1)} fusion(bf16[1056,3200]{1,0:T(8,128)(2,1)} %bitcast.55, s32[]{:T(128)S(6)} %select_n.97), kind=kLoop, calls=%fused_computation.77 | loop fusion | bytes 3180804 | tf_op jit(solution)/shard_map/slice | solution.py:398
  180.7 0.1 fusion.26
  180.8 0.8 dynamic_slice.7
  181.6 2.3 copy.36
  183.9 2.8 copy.37
  186.7 0.5 convert_element_type.47.valid_ref
  187.2 4.9 %dynamic-slice_select_fusion = bf16[1024,800]{1,0:T(8,128)(2,1)} fusion(bf16[1056,3200]{1,0:T(8,128)(2,1)} %bitcast.56, s32[]{:T(128)S(6)} %add.76, s32[]{:T(128)S(6)} %select_n.97, bf16[994,800]{1,0:T(8,128)(2,1)} %constant_dynamic-slice_fusion, bf16[31,800]{1,0:T(8,128)(2,1)S(1)} %collective-permute-done.4, pred[]{:T(512)S(6)} %lt.85), kind=kLoop, calls=%fused_computation.14 | loop fusion | flops 4096000 | bytes 4916809 | tf_op jit(solution)/shard_map/jit(_where)/select_n | solution.py:399
  192.1 4.8 %reshape.206 = bf16[16,2,16,2,800]{4,3,2,1,0:T(2,128)(2,1)} reshape(bf16[1024,800]{1,0:T(8,128)(2,1)} %dynamic-slice_select_fusion) | data formatting | bytes 3276800 | tf_op jit(solution)/shard_map/reshape | solution.py:22
  196.9 3.0 copy.38
  199.9 7.6 %reshape_reshape.3 = bf16[4,256,2,400]{3,2,1,0:T(2,128)(2,1)} reshape(bf16[2,2,16,16,800]{4,3,2,1,0:T(8,128)(2,1)} %copy.38) | data formatting | bytes 3276800 | tf_op jit(solution)/shard_map/reshape;reshape | solution.py:464
  207.5 3.3 %copy.42 = bf16[4,256,2,400]{3,1,0,2:T(8,128)(2,1)} copy(bf16[4,256,2,400]{3,2,1,0:T(2,128)(2,1)} %reshape_reshape.3) | data formatting | bytes 3276800 | tf_op jit(solution)/shard_map/reshape;reshape | solution.py:464
  210.8 1.6 copy-done
  212.4 1.6 copy-done.2
  214.0 9.9 %project_merge.1.merged_ref = bf16[2,256,1600]{2,1,0:T(8,128)(2,1)S(1)} custom-call(bf16[4,4,256,256]{3,2,1,0:T(8,128)(2,1)S(1)} %bitcast.53, bf16[2,8,128,400]{3,2,1,0:T(8,128)(2,1)S(1)} %bitcast.51, bf16[2,4,256,400]{3,2,1,0:T(8,128)(2,1)S(1)} %bitcast.52, f32[2,1,400]{2,1,0:T(1,128)S(1)} %reshape.207.scale_ref), custom_call_target="tpu_custom_call" | custom-call | tf_op jit(solution)/shard_map/project_merge/pallas_call | solution.py:61
  223.9 1.2 copy-done.1
  225.1 84.6 %deliver.1 = bf16[4,2,256,1600]{3,2,1,0:T(8,128)(2,1)} custom-call(bf16[2,256,1600]{2,1,0:T(8,128)(2,1)} %copy-done.1), custom_call_target="tpu_custom_call" | custom-call | tf_op jit(solution)/shard_map/deliver/pallas_call | solution.py:315
  309.7 4.1 %place_tiles.1 = bf16[4,256,1600]{2,1,0:T(8,128)(2,1)} custom-call(s32[4]{0:T(128)} %select_reduce_fusion.1.tile_ref, s32[4]{0:T(128)} %convert_element_type.47.valid_ref, bf16[8,256,1600]{2,1,0:T(8,128)(2,1)} %bitcast.59), custom_call_target="tpu_custom_call" | custom-call | tf_op jit(solution)/shard_map/place_tiles/pallas_call | solution.py:347
  313.8 5.5 %copy.40 = bf16[4,256,1600]{1,2,0:T(8,128)(2,1)} copy(bf16[4,256,1600]{2,1,0:T(8,128)(2,1)} %place_tiles.1) | data formatting | bytes 6553600 | tf_op jit(solution)/shard_map/place_tiles/pallas_call | solution.py:347
  (63 shorter events, 0.8 us)
Async XLA Ops:
  6.5 204.2 %all-gather.2.cloned.1.call-start = ((), (), s32[]{:S(2)}) async-start(), calls=%async_computation | async-start | bytes 2621440 | tf_op jit(solution)/shard_map/all_gather | solution.py:455
  110.2 4.5 %copy-start.3 = (bf16[2,4,800,384]{3,2,1,0:T(8,128)(2,1)S(1)}, bf16[2,4,800,384]{3,2,1,0:T(8,128)(2,1)}, u32[]{:S(2)}) copy-start(bf16[2,4,800,384]{3,2,1,0:T(8,128)(2,1)} %get-tuple-element.9) | copy-start | bytes 14745604
  110.2 6.5 %slice-start = ((s8[6758400]{0:T(1024)(128)(4,1)}), s8[4194304]{0:T(1024)(128)(4,1)S(1)}, s32[]{:S(2)}) async-start(s8[6758400]{0:T(1024)(128)(4,1)} %bitcast.57), calls=%async_computation.1 | async-start | bytes 8388608
  114.7 2.8 slice-start.1
  114.8 2.8 copy-start.7
  125.4 31.4 %copy-start.5 = (bf16[1056,384]{1,0:T(8,128)(2,1)}, bf16[1056,384]{1,0:T(8,128)(2,1)S(1)}, u32[]{:S(2)}) copy-start(bf16[1056,384]{1,0:T(8,128)(2,1)S(1)} %get-tuple-element.43) | copy-start | bytes 2433028
  125.5 4.6 %copy-start.8 = (f32[2,128]{1,0:T(2,128)S(1)}, f32[2,128]{1,0:T(2,128)}, u32[]{:S(2)}) copy-start(f32[2,128]{1,0:T(2,128)} %param.11) | copy-start | bytes 3076
  129.2 27.7 %copy-start.6 = (bf16[1056,384]{1,0:T(8,128)(2,1)}, bf16[1056,384]{1,0:T(8,128)(2,1)S(1)}, u32[]{:S(2)}) copy-start(bf16[1056,384]{1,0:T(8,128)(2,1)S(1)} %get-tuple-element.41) | copy-start | bytes 2433028
  130.0 12.4 %collective-permute-start = (f32[2,1056]{1,0:T(2,128)S(1)}, f32[2,1056]{1,0:T(2,128)S(1)}, u32[]{:S(2)}, u32[]{:S(2)}) collective-permute-start(f32[2,1056]{1,0:T(2,128)S(1)} %pad_maximum_fusion.19), channel_id=1, source_target_pairs={{0,1},{1,0},{2,3},{3,2},{4,5},{5,4},{6,7},{7,6},{8,9},{9,8},{10,11... | collective-permute-start | bytes 25352 | tf_op jit(solution)/shard_map/ppermute | solution.py:421
  130.1 20.7 %collective-permute-start.2 = (f32[2,128]{1,0:T(2,128)S(1)}, f32[2,128]{1,0:T(2,128)S(1)}, u32[]{:S(2)}, u32[]{:S(2)}) collective-permute-start(f32[2,128]{1,0:T(2,128)S(1)} %copy-done.8), channel_id=1, source_target_pairs={{0,4},{1,5},{2,6},{3,7},{4,0},{5,1},{6,2},{7,3},{8,12},{9,13},{10,... | collective-permute-start | bytes 3080 | tf_op jit(solution)/shard_map/ppermute | solution.py:393
  142.4 10.0 %collective-permute-start.1 = (f32[2,1056]{1,0:T(2,128)S(1)}, f32[2,1056]{1,0:T(2,128)S(1)}, u32[]{:S(2)}, u32[]{:S(2)}) collective-permute-start(f32[2,1056]{1,0:T(2,128)S(1)} %fusion.37), channel_id=1, source_target_pairs={{0,2},{1,3},{2,0},{3,1},{4,6},{5,7},{6,4},{7,5},{8,10},{9,11},{10,... | collective-permute-start | bytes 25352 | tf_op jit(solution)/shard_map/ppermute | solution.py:421
  152.9 5.5 %collective-permute-start.3 = (bf16[31,768]{1,0:T(8,128)(2,1)S(1)}, bf16[31,768]{1,0:T(8,128)(2,1)S(1)}, u32[]{:S(2)}, u32[]{:S(2)}) collective-permute-start(bf16[31,768]{1,0:T(8,128)(2,1)S(1)} %constant_dynamic-update-slice_fusion), channel_id=1, source_target_pairs={{0,4},{1,5},{2,6},{3,7},{8,12},{9,13},{10,14},{11,15},{16,20},{17,... | collective-permute-start | bytes 142856 | tf_op jit(solution)/shard_map/ppermute | solution.py:432
  168.4 7.6 %copy-start.9 = (s32[4,2]{0,1:T(2,128)S(1)}, s32[4,2]{0,1:T(2,128)}, u32[]{:S(2)}) copy-start(s32[4,2]{0,1:T(2,128)} %param.15) | copy-start | bytes 100
  168.4 7.6 %copy-start.10 = (s32[4,2]{0,1:T(2,128)S(1)}, s32[4,2]{0,1:T(2,128)}, u32[]{:S(2)}) copy-start(s32[4,2]{0,1:T(2,128)} %param.14) | copy-start | bytes 100
  168.4 13.2 %copy-start.4 = (bf16[8,128,800]{2,1,0:T(8,128)(2,1)S(1)}, bf16[8,128,800]{2,1,0:T(8,128)(2,1)}, u32[]{:S(2)}) copy-start(bf16[8,128,800]{2,1,0:T(8,128)(2,1)} %get-tuple-element.10) | copy-start | bytes 4915204
  170.6 16.6 %collective-permute-start.4 = (bf16[31,800]{1,0:T(8,128)(2,1)S(1)}, bf16[31,800]{1,0:T(8,128)(2,1)S(1)}, u32[]{:S(2)}, u32[]{:S(2)}) collective-permute-start(bf16[31,800]{1,0:T(8,128)(2,1)S(1)} %dynamic-slice.1), channel_id=1, source_target_pairs={{0,4},{1,5},{2,6},{3,7},{8,12},{9,13},{10,14},{11,15},{16,20},{17,... | collective-permute-start | bytes 148808 | tf_op jit(solution)/shard_map/ppermute | solution.py:462
  210.8 1.6 copy-start
  212.4 1.6 copy-start.2
  223.9 1.2 copy-start.1
Sparse Core Ops, SparseCore 0:
  169.8 31.6 all-gather.1
